TPU v7x, 32 devices: a whole 2x2x4 slice. The times are simulated.
32 devices in a mesh: blk: 8 (over y, x, core), tm: 4 (over z).
Axes of the slice: x: 2, y: 2, z: 4, core: 2. Of those that a mesh axis runs over, the one named last changes fastest.
Arguments:
- records: bfloat16 [2048, 16, 512], P('blk', 'tm'), may hold values from -6 to 6
- glitch_mask: int32 [2048, 16], P('blk'), may hold values 0 or 1
- fir_taps: bfloat16 [65], replicated, may hold values from -1.1953125 to 1.1953125
Outputs:
- correlations: bfloat16 [16, 2048, 2048], P('tm', 'blk')
All inputs are finite; a program needn't handle non-finite values. No bound on the sum of `glitch_mask` on one device may be relied on, other than what follows from the above.
Results may differ from a plain program's by a relative error of at most 0.015.
Values may be sent and summed in bfloat16 or wider, within the bound.
A program may use at most 256 MiB of HBM per device.

v0:
```python
import math
import jax
import jax.numpy as jnp
import numpy as np
from jax import lax
from jax.sharding import PartitionSpec as P

BINS = 128
FIRST_BIN = 16
SMOOTH = 64
LAGS = 16


def dft_thirds(seglen):
    sample = np.arange(seglen)[:, None]
    freq = np.arange(BINS)[None, :] + FIRST_BIN
    angle = sample * freq % seglen * (2.0 * math.pi / seglen)
    rest = np.concatenate([np.cos(angle), -np.sin(angle)], axis=1).astype(np.float32)
    thirds = []
    for _ in range(3):
        part = rest.astype(jnp.bfloat16)
        thirds.append(part)
        rest = rest - part.astype(np.float32)
    return np.concatenate(thirds, axis=1)


def lag_rows(seg_total, seglen):
    delay = np.arange(LAGS)[:, None] - LAGS // 2
    freq = np.arange(BINS)[None, :] + FIRST_BIN
    angle = delay * freq % seglen * (2.0 * math.pi / seglen)
    factor = 1.0 / math.sqrt(seg_total * BINS)
    tables = np.stack([np.cos(angle), np.sin(angle)]).astype(np.float32) * np.float32(factor)
    return tables.astype(jnp.bfloat16).astype(np.float32)


def filter_matrix(fir_taps, seglen):
    half = (fir_taps.shape[0] - 1) // 2
    period = 2 * seglen
    line = jnp.pad(fir_taps[::-1], (seglen - 1 - half, seglen - half))
    rows = jnp.tile(line, seglen)[: seglen * (period - 1)].reshape(seglen, period - 1)
    return rows[:, seglen - 1 :]


def transform_table(fir_taps, seglen):
    parts = jnp.dot(
        filter_matrix(fir_taps, seglen),
        jnp.asarray(dft_thirds(seglen)),
        preferred_element_type=jnp.float32,
    )
    width = 2 * BINS
    total = parts[:, :width] + (parts[:, width : 2 * width] + parts[:, 2 * width :])
    return total.astype(jnp.bfloat16)


def whiten(samples, usable, fir_taps):
    seglen = samples.shape[1]
    source = lax.broadcasted_iota(jnp.int32, (seglen, seglen), 0)
    target = lax.broadcasted_iota(jnp.int32, (seglen, seglen), 1)
    band_ones = jnp.where(jnp.abs(source - target) <= SMOOTH, 1.0, 0.0).astype(jnp.bfloat16)
    where = lax.broadcasted_iota(jnp.int32, (1, seglen), 1)
    counts = jnp.minimum(where, SMOOTH) + jnp.minimum(seglen - 1 - where, SMOOTH) + 1
    envelope = jnp.dot(
        jnp.abs(samples), band_ones, preferred_element_type=jnp.float32
    ) / counts.astype(jnp.float32)
    normal = (samples.astype(jnp.float32) / (envelope + 1e-06)).astype(jnp.bfloat16)
    spectra = jnp.dot(normal, transform_table(fir_taps, seglen), preferred_element_type=jnp.float32)
    power = jnp.sum(spectra * spectra, axis=1, keepdims=True) * jnp.float32(1.0 / BINS)
    scale = usable.astype(jnp.float32)[:, None] / jnp.sqrt(power + 1e-06)
    return (spectra * scale).astype(jnp.bfloat16)


def body(records, glitch_mask, fir_taps):
    tm_count = lax.axis_size("tm")
    tm_index = lax.axis_index("tm")
    chans, segs, seglen = records.shape
    seg_total = glitch_mask.shape[1]
    usable = lax.dynamic_slice_in_dim(glitch_mask, tm_index * segs, segs, 1)
    white = whiten(records.reshape(chans * segs, seglen), usable.reshape(chans * segs), fir_taps)
    slab = white.reshape(chans, segs * 2 * BINS)
    column = lax.all_gather(slab, "tm", axis=1, tiled=True)
    every = lax.all_gather(column, "blk", axis=0, tiled=True)
    lags_dev = LAGS // tm_count
    tables = lax.dynamic_slice_in_dim(
        jnp.asarray(lag_rows(seg_total, seglen)), tm_index * lags_dev, lags_dev, 1
    )
    cos_rows = tables[0][:, None, None, :]
    sin_rows = tables[1][:, None, None, :]
    own = column.reshape(chans, seg_total, 2, BINS).astype(jnp.float32)
    real_part, imag_part = (own[None, :, :, 0], own[None, :, :, 1])
    turned = jnp.stack(
        [cos_rows * real_part - sin_rows * imag_part, cos_rows * imag_part + sin_rows * real_part],
        axis=3,
    ).astype(jnp.bfloat16)
    left = turned.reshape(lags_dev, chans, seg_total * 2 * BINS)
    return jnp.einsum("lik,jk->lij", left, every, preferred_element_type=jnp.float32).astype(
        jnp.bfloat16
    )


def solution(mesh):
    placed = (P("blk", "tm", None), P("blk", None), P())
    return jax.shard_map(
        body, mesh=mesh, in_specs=placed, out_specs=P("tm", "blk", None), check_vma=False
    )
```

profile of v0, /device:TPU:0, one launch (start us, length us, event | category | flops | bytes accessed | tf_op | source)
XLA Modules:
  0.0 192.0 jit_solution(9935563108440876466)
XLA Ops:
  6.5 0.0 all-gather.3.cloned.1.call-start
  6.5 1.8 abs.10
  8.3 2.4 %reshape.75 = f32[1024,512]{1,0:T(8,128)} reshape(bf16[256,4,512]{2,1,0:T(4,128)(2,1)} %param.5) | data formatting | bytes 3145728 | tf_op jit(solution)/shard_map/convert_element_type | solution.py:65
  10.7 0.7 dynamic-slice_convert_fusion
  11.4 0.1 copy.6
  11.6 0.1 convert_element_type.59
  11.7 0.7 rev.3
  12.5 0.1 pad.4
  12.5 0.2 broadcast_bitcast_fusion
  12.8 0.3 copy.8
  13.1 1.6 reshape.73
  14.7 1.1 abs.11
  15.8 1.7 fusion.11
  17.6 3.1 %multiply_reduce_fusion = (f32[1024]{0:T(1024)S(1)}, f32[1024,256]{0,1:T(8,128)S(1)}) fusion(f32[512,768]{1,0:T(8,128)S(1)} %fusion.11, f32[1024,512]{1,0:T(8,128)} %reshape.75, bf16[1024,512]{1,0:T(8,128)(2,1)} %abs.11, f32[512]{0:T(512)S(1)} %fusion.22), kind=kOutput, calls=%fused_computation.10 | convolution fusion | flops 809630720 | bytes 5773312 | tf_op jit(solution)/shard_map/dot_general | solution.py:66
  20.7 0.1 multiply_convert_fusion
  20.8 0.2 copy.7
  21.0 1.1 reshape.74
  22.1 0.0 all-gather.3.cloned.1.call-update
  22.1 0.2 all-gather.5.cloned.1.call-start
  22.3 48.6 %all-gather.3.cloned.1.call-done = bf16[256,4096]{1,0:T(8,128)(2,1)} async-done(((bf16[256,1024]{1,0:T(8,128)(2,1)}), bf16[256,4096]{1,0:T(8,128)(2,1)}) %all-gather.3.cloned.1.call-update) | async-done | bytes 2097168 | tf_op jit(solution)/shard_map/all_gather | solution.py:80
  70.9 0.0 all-gather.5.cloned.1.call-update
  70.9 0.7 dynamic-slice_bitcast_fusion.1
  71.7 6.6 %reshape.76 = f32[256,16,2,128]{3,2,1,0:T(2,128)} reshape(bf16[256,4096]{1,0:T(8,128)(2,1)} %all-gather.3.cloned.1.call-done) | data formatting | bytes 6291456 | tf_op jit(solution)/shard_map/convert_element_type | solution.py:88
  78.2 10.3 %fusion.31 = (f32[256,16,1,128]{3,2,1,0:T(1,128)S(1)}, f32[256,16,1,128]{3,2,1,0:T(1,128)}) fusion(f32[256,16,2,128]{3,2,1,0:T(2,128)} %reshape.76), kind=kLoop, calls=%fused_computation.38 | loop fusion | bytes 8388608 | tf_op jit(solution)/shard_map/slice | solution.py:89
  88.5 18.6 %subtract_convert_fusion = (bf16[4,256,16,1,128]{4,3,2,1,0:T(2,128)(2,1)S(1)}, bf16[4,256,16,1,128]{4,3,2,1,0:T(2,128)(2,1)S(1)}) fusion(f32[256,16,128]{2,1,0:T(8,128)} %bitcast.27, f32[4,128]{1,0:T(4,128)S(1)} %get-tuple-element.10, f32[256,16,128]{2,1,0:T(8,128)S(1)} %bitcast.26, f32[4,128]{1,0:T(4,128)S(1)} %get-tuple-element.9), kind=kLoop, calls=%fused_computation.4 | loop fusion | flops 16777216 | bytes 12587008 | tf_op jit(solution)/shard_map/convert.2
  107.2 20.3 %pad_maximum_fusion = bf16[4,256,16,2,128]{4,3,2,1,0:T(2,128)(2,1)} fusion(bf16[4,256,16,1,128]{4,3,2,1,0:T(2,128)(2,1)S(1)} %get-tuple-element.6, bf16[4,256,16,1,128]{4,3,2,1,0:T(2,128)(2,1)S(1)} %get-tuple-element.5), kind=kLoop, calls=%fused_computation.2 | loop fusion | flops 16777216 | bytes 16777216 | tf_op jit(solution)/shard_map/stack | solution.py:90
  127.5 14.5 %convert_element_type.63 = bf16[4,256,4096]{2,1,0:T(8,128)(2,1)} reshape(bf16[4,256,16,2,128]{4,3,2,1,0:T(2,128)(2,1)} %pad_maximum_fusion) | data formatting | bytes 16777216 | tf_op jit(solution)/shard_map/convert_element_type | solution.py:93
  142.0 19.4 %all-gather.5.cloned.1.call-done = bf16[2048,4096]{1,0:T(8,128)(2,1)} async-done(((bf16[256,4096]{1,0:T(8,128)(2,1)}), bf16[2048,4096]{1,0:T(8,128)(2,1)}) %all-gather.5.cloned.1.call-update) | async-done | bytes 16777232 | tf_op jit(solution)/shard_map/all_gather | solution.py:81
  161.4 23.8 %fusion.2 = bf16[4,256,2048]{2,1,0:T(8,128)(2,1)} fusion(bf16[4,256,4096]{2,1,0:T(8,128)(2,1)} %convert_element_type.63, bf16[2048,4096]{1,0:T(8,128)(2,1)} %all-gather.5.cloned.1.call-done), kind=kOutput, calls=%fused_computation.5 | convolution fusion | flops 17181966336 | bytes 29360128 | tf_op jit(solution)/shard_map/lik,jk->lij/dot_general | solution.py:95
  (2 shorter events, 0.0 us)
Async XLA Ops:
  6.5 64.4 %all-gather.3.cloned.1.call-start = ((), (), s32[]{:S(2)}) async-start(), calls=%async_computation | async-start | bytes 2621440 | tf_op jit(solution)/shard_map/all_gather | solution.py:80
  22.1 139.3 %all-gather.5.cloned.1.call-start = ((), (), s32[]{:S(2)}) async-start(), calls=%async_computation.1 | async-start | bytes 18874368 | tf_op jit(solution)/shard_map/all_gather | solution.py:81
Sparse Core Ops, SparseCore 0:
  22.2 48.6 all-gather.2
  72.8 88.5 all-gather.4
where the time goes:
time: 193 us; the launch traced here: 192 us
  waiting for transfers between devices  68 us (35%)
  other arithmetic  41.5 us (22%)
  local copies, waits for them, and re-layouts  40.2 us (21%)
  matrix products  28.6 us (15%)
  between operations  13.5 us (7%)
    all_gather x1, waiting for transfers between devices, body(): column = lax.all_gather(slab, 'tm', axis=1, tiled=True)  48.6 us
    dot_general x1, matrix products, body(): jnp.einsum('lik,jk->lij', left, every, preferred_element_type=jnp.float32)  23.8 us
    another operation x1, other arithmetic, body(): jnp.stack([cos_rows * real_part - sin_rows * imag_part, cos_rows * imag_p...  20.3 us
    all_gather x1, waiting for transfers between devices, body(): every = lax.all_gather(column, 'blk', axis=0, tiled=True)  19.4 us
    another operation x1, other arithmetic  18.6 us
    convert_element_type x1, local copies, waits for them, and re-layouts, body(): turned = jnp.stack([cos_rows * real_part - sin_rows * imag_part, cos_rows...  14.5 us
    slice x1, local copies, waits for them, and re-layouts, body(): real_part, imag_part = (own[None, :, :, 0], own[None, :, :, 1])  10.3 us
    convert_element_type x1, local copies, waits for them, and re-layouts, body(): own = column.reshape(chans, seg_total, 2, BINS).astype(jnp.float32)  6.6 us
  transfers between devices with their start and end apart: 2, of which 2 were waited for; matrix products, arithmetic and copies ran while one was open for 37% of the time, Pallas kernels for 0%

commit v1 on v0

--- a/solution.py
+++ b/solution.py
@@ -78,7 +78,16 @@
     white = whiten(records.reshape(chans * segs, seglen), usable.reshape(chans * segs), fir_taps)
     slab = white.reshape(chans, segs * 2 * BINS)
     column = lax.all_gather(slab, "tm", axis=1, tiled=True)
-    every = lax.all_gather(column, "blk", axis=0, tiled=True)
+    peers, index, rows_2 = (lax.axis_size("blk"), lax.axis_index("blk"), column.shape[0])
+    right = [(i, (i + 1) % peers) for i in range(peers)]
+    filled = jnp.zeros((*column.shape[:0], peers * rows_2, *column.shape[0 + 1 :]), column.dtype)
+    held = column
+    for step in range(peers):
+        owner = (index - step) % peers
+        filled = lax.dynamic_update_slice_in_dim(filled, held, owner * rows_2, axis=0)
+        if step < peers - 1:
+            held = lax.ppermute(held, "blk", right)
+    every = filled
     lags_dev = LAGS // tm_count
     tables = lax.dynamic_slice_in_dim(
         jnp.asarray(lag_rows(seg_total, seglen)), tm_index * lags_dev, lags_dev, 1

time: 193 us -> 296 us (1.53)
  waiting for transfers between devices: 68 us -> 164 us
  local copies, waits for them, and re-layouts: 40.2 us -> 52.1 us
  matrix products: 28.6 us -> 23.9 us
    ppermute x0 -> x7, waiting for transfers between devices: none -> 115 us  [body(): held = lax.ppermute(held, 'blk', right)]
    all_gather x1 -> x0, waiting for transfers between devices: 19.4 us -> none  [body(): every = lax.all_gather(column, 'blk', axis=0, tiled=True)]
    dynamic_update_slice x0 -> x8, local copies, waits for them, and re-layouts: none -> 8.8 us  [body(): lax.dynamic_update_slice_in_dim(filled, held, owner * rows_2, axis=0)]
    dot_general x1, matrix products: 23.8 us -> 19 us  [body(): jnp.einsum('lik,jk->lij', left, every, preferred_element_type=jnp.float32)]
  transfers between devices with their start and end apart: 2 -> 8, of which waited for: 2 -> 7; matrix products, arithmetic and copies ran while one was open for 37% -> 27% of each run, Pallas kernels for 0% -> 0%
where the time goes in v1:
time: 296 us; the launch traced here: 295 us
  waiting for transfers between devices  164 us (55%)
  local copies, waits for them, and re-layouts  52.1 us (18%)
  other arithmetic  41.4 us (14%)
  matrix products  23.9 us (8%)
  between operations  13.6 us (5%)
    ppermute x7, waiting for transfers between devices, body(): held = lax.ppermute(held, 'blk', right)  115 us
    all_gather x1, waiting for transfers between devices, body(): column = lax.all_gather(slab, 'tm', axis=1, tiled=True)  48.8 us
    another operation x1, other arithmetic, body(): jnp.stack([cos_rows * real_part - sin_rows * imag_part, cos_rows * imag_p...  20.2 us
    dot_general x1, matrix products, body(): jnp.einsum('lik,jk->lij', left, every, preferred_element_type=jnp.float32)  19 us
    another operation x1, other arithmetic  18.6 us
    convert_element_type x1, local copies, waits for them, and re-layouts, body(): turned = jnp.stack([cos_rows * real_part - sin_rows * imag_part, cos_rows...  14.4 us
    slice x1, local copies, waits for them, and re-layouts, body(): real_part, imag_part = (own[None, :, :, 0], own[None, :, :, 1])  9.11 us
    dynamic_update_slice x8, local copies, waits for them, and re-layouts, body(): lax.dynamic_update_slice_in_dim(filled, held, owner * rows_2, axis=0)  8.8 us
  transfers between devices with their start and end apart: 8, of which 7 were waited for; matrix products, arithmetic and copies ran while one was open for 27% of the time, Pallas kernels for 0%

profile of v1, /device:TPU:0, one launch (start us, length us, event | category | flops | bytes accessed | tf_op | source)
XLA Modules:
  0.0 295.0 jit_solution(9926172988491476801)
XLA Ops:
  6.5 1.8 abs.10
  8.3 2.4 reshape.75
  10.7 0.7 dynamic-slice_convert_fusion
  11.7 0.7 rev.3
  13.1 1.6 reshape.73
  14.7 1.1 abs.11
  15.8 1.7 fusion.11
  17.6 3.1 %multiply_reduce_fusion = (f32[1024]{0:T(1024)S(1)}, f32[1024,256]{0,1:T(8,128)S(1)}) fusion(f32[512,768]{1,0:T(8,128)S(1)} %fusion.11, f32[1024,512]{1,0:T(8,128)} %reshape.75, bf16[1024,512]{1,0:T(8,128)(2,1)} %abs.11, f32[512]{0:T(512)S(1)} %fusion.24), kind=kOutput, calls=%fused_computation.10 | convolution fusion | flops 809630720 | bytes 5773312 | tf_op jit(solution)/shard_map/dot_general | solution.py:66
  21.0 1.1 reshape.74
  22.1 48.8 %all-gather.2.cloned.1.call-done = bf16[256,4096]{1,0:T(8,128)(2,1)} async-done(((bf16[256,1024]{1,0:T(8,128)(2,1)}), bf16[256,4096]{1,0:T(8,128)(2,1)}) %all-gather.2.cloned.1.call-update) | async-done | bytes 2097168 | tf_op jit(solution)/shard_map/all_gather | solution.py:80
  70.9 26.6 %collective-permute-done = bf16[256,4096]{1,0:T(8,128)(2,1)S(1)} collective-permute-done((bf16[256,4096]{1,0:T(8,128)(2,1)}, bf16[256,4096]{1,0:T(8,128)(2,1)S(1)}, u32[]{:S(2)}, u32[]{:S(2)}) %collective-permute-start) | collective-permute-done | bytes 2097184 | tf_op jit(solution)/shard_map/ppermute | solution.py:89
  97.5 26.4 %collective-permute-done.1 = bf16[256,4096]{1,0:T(8,128)(2,1)S(1)} collective-permute-done((bf16[256,4096]{1,0:T(8,128)(2,1)S(1)}, bf16[256,4096]{1,0:T(8,128)(2,1)S(1)}, u32[]{:S(2)}, u32[]{:S(2)}) %collective-permute-start.1) | collective-permute-done | bytes 2097184 | tf_op jit(solution)/shard_map/ppermute | solution.py:89
  123.9 1.4 copy-done.1
  125.2 26.5 %collective-permute-done.2 = bf16[256,4096]{1,0:T(8,128)(2,1)} collective-permute-done((bf16[256,4096]{1,0:T(8,128)(2,1)S(1)}, bf16[256,4096]{1,0:T(8,128)(2,1)}, u32[]{:S(2)}, u32[]{:S(2)}) %collective-permute-start.2) | collective-permute-done | bytes 2097184 | tf_op jit(solution)/shard_map/ppermute | solution.py:89
  151.7 0.7 fusion.21
  152.4 6.6 %reshape.76 = f32[256,16,2,128]{3,2,1,0:T(2,128)} reshape(bf16[256,4096]{1,0:T(8,128)(2,1)} %all-gather.2.cloned.1.call-done) | data formatting | bytes 6291456 | tf_op jit(solution)/shard_map/convert_element_type | solution.py:97
  159.0 9.1 %fusion.33 = (f32[256,16,1,128]{3,2,1,0:T(1,128)S(1)}, f32[256,16,1,128]{3,2,1,0:T(1,128)}) fusion(f32[256,16,2,128]{3,2,1,0:T(2,128)} %reshape.76), kind=kLoop, calls=%fused_computation.48 | loop fusion | bytes 8388608 | tf_op jit(solution)/shard_map/slice | solution.py:98
  168.1 10.3 %collective-permute-done.3 = bf16[256,4096]{1,0:T(8,128)(2,1)} collective-permute-done((bf16[256,4096]{1,0:T(8,128)(2,1)}, bf16[256,4096]{1,0:T(8,128)(2,1)}, u32[]{:S(2)}, u32[]{:S(2)}) %collective-permute-start.3) | collective-permute-done | bytes 2097184 | tf_op jit(solution)/shard_map/ppermute | solution.py:89
  178.4 18.6 %subtract_convert_fusion = (bf16[4,256,16,1,128]{4,3,2,1,0:T(2,128)(2,1)S(1)}, bf16[4,256,16,1,128]{4,3,2,1,0:T(2,128)(2,1)S(1)}) fusion(f32[256,16,128]{2,1,0:T(8,128)} %bitcast.29, f32[4,128]{1,0:T(4,128)S(1)} %get-tuple-element.10, f32[256,16,128]{2,1,0:T(8,128)S(1)} %bitcast.28, f32[4,128]{1,0:T(4,128)S(1)} %get-tuple-element.9), kind=kLoop, calls=%fused_computation.4 | loop fusion | flops 16777216 | bytes 12587008 | tf_op jit(solution)/shard_map/convert.2
  197.0 8.0 %collective-permute-done.4 = bf16[256,4096]{1,0:T(8,128)(2,1)} collective-permute-done((bf16[256,4096]{1,0:T(8,128)(2,1)}, bf16[256,4096]{1,0:T(8,128)(2,1)}, u32[]{:S(2)}, u32[]{:S(2)}) %collective-permute-start.4) | collective-permute-done | bytes 2097184 | tf_op jit(solution)/shard_map/ppermute | solution.py:89
  205.0 20.2 %pad_maximum_fusion = bf16[4,256,16,2,128]{4,3,2,1,0:T(2,128)(2,1)} fusion(bf16[4,256,16,1,128]{4,3,2,1,0:T(2,128)(2,1)S(1)} %get-tuple-element.6, bf16[4,256,16,1,128]{4,3,2,1,0:T(2,128)(2,1)S(1)} %get-tuple-element.5), kind=kLoop, calls=%fused_computation.2 | loop fusion | flops 16777216 | bytes 16777216 | tf_op jit(solution)/shard_map/stack | solution.py:99
  225.2 14.4 %convert_element_type.63 = bf16[4,256,4096]{2,1,0:T(8,128)(2,1)} reshape(bf16[4,256,16,2,128]{4,3,2,1,0:T(2,128)(2,1)} %pad_maximum_fusion) | data formatting | bytes 16777216 | tf_op jit(solution)/shard_map/convert_element_type | solution.py:102
  239.7 1.9 broadcast_in_dim.15
  241.6 0.3 constant_dynamic-update-slice_fusion.7
  241.9 0.3 constant_dynamic-update-slice_fusion.6
  242.3 1.0 copy-done.2
  243.6 1.9 constant_dynamic-update-slice_fusion.4
  245.4 2.0 constant_dynamic-update-slice_fusion.3
  247.4 1.9 constant_dynamic-update-slice_fusion.2
  249.3 2.0 constant_dynamic-update-slice_fusion.1
  251.3 17.5 %collective-permute-done.6 = bf16[256,4096]{1,0:T(8,128)(2,1)S(1)} collective-permute-done((bf16[256,4096]{1,0:T(8,128)(2,1)}, bf16[256,4096]{1,0:T(8,128)(2,1)S(1)}, u32[]{:S(2)}, u32[]{:S(2)}) %collective-permute-start.6) | collective-permute-done | bytes 2097184 | tf_op jit(solution)/shard_map/ppermute | solution.py:89
  269.1 19.0 %fusion.2 = bf16[4,256,2048]{2,1,0:T(8,128)(2,1)} fusion(bf16[4,256,4096]{2,1,0:T(8,128)(2,1)S(1)} %bitcast.27, bf16[2048,4096]{1,0:T(8,128)(2,1)S(1)} %constant_dynamic-update-slice_fusion), kind=kOutput, calls=%fused_computation.5 | convolution fusion | flops 17181966336 | bytes 29360128 | tf_op jit(solution)/shard_map/lik,jk->lij/dot_general | solution.py:104
  (34 shorter events, 1.8 us)
Async XLA Ops:
  6.5 64.4 %all-gather.2.cloned.1.call-start = ((), (), s32[]{:S(2)}) async-start(), calls=%async_computation | async-start | bytes 2621440 | tf_op jit(solution)/shard_map/all_gather | solution.py:80
  70.9 26.6 %collective-permute-start = (bf16[256,4096]{1,0:T(8,128)(2,1)}, bf16[256,4096]{1,0:T(8,128)(2,1)S(1)}, u32[]{:S(2)}, u32[]{:S(2)}) collective-permute-start(bf16[256,4096]{1,0:T(8,128)(2,1)} %all-gather.2.cloned.1.call-done), channel_id=1, source_target_pairs={{0,4},{4,8},{8,12},{12,16},{16,20},{20,24},{24,28},{28,0},{1,5},{5... | collective-permute-start | bytes 6291464 | tf_op jit(solution)/shard_map/ppermute | solution.py:89
  97.5 54.2 %copy-start.3 = (bf16[256,4096]{1,0:T(8,128)(2,1)}, bf16[256,4096]{1,0:T(8,128)(2,1)S(1)}, u32[]{:S(2)}) copy-start(bf16[256,4096]{1,0:T(8,128)(2,1)S(1)} %collective-permute-done) | copy-start | bytes 6291460
  97.5 26.4 %collective-permute-start.1 = (bf16[256,4096]{1,0:T(8,128)(2,1)S(1)}, bf16[256,4096]{1,0:T(8,128)(2,1)S(1)}, u32[]{:S(2)}, u32[]{:S(2)}) collective-permute-start(bf16[256,4096]{1,0:T(8,128)(2,1)S(1)} %collective-permute-done), channel_id=1, source_target_pairs={{0,4},{4,8},{8,12},{12,16},{16,20},{20,24},{24,28},{28,0},{1,5},{5... | collective-permute-start | bytes 6291464 | tf_op jit(solution)/shard_map/ppermute | solution.py:89
  123.9 1.4 copy-start.1
  125.2 26.5 %collective-permute-start.2 = (bf16[256,4096]{1,0:T(8,128)(2,1)S(1)}, bf16[256,4096]{1,0:T(8,128)(2,1)}, u32[]{:S(2)}, u32[]{:S(2)}) collective-permute-start(bf16[256,4096]{1,0:T(8,128)(2,1)S(1)} %collective-permute-done.1), channel_id=1, source_target_pairs={{0,4},{4,8},{8,12},{12,16},{16,20},{20,24},{24,28},{28,0},{1,5},{5... | collective-permute-start | bytes 6291464 | tf_op jit(solution)/shard_map/ppermute | solution.py:89
  151.7 26.7 %collective-permute-start.3 = (bf16[256,4096]{1,0:T(8,128)(2,1)}, bf16[256,4096]{1,0:T(8,128)(2,1)}, u32[]{:S(2)}, u32[]{:S(2)}) collective-permute-start(bf16[256,4096]{1,0:T(8,128)(2,1)} %collective-permute-done.2), channel_id=1, source_target_pairs={{0,4},{4,8},{8,12},{12,16},{16,20},{20,24},{24,28},{28,0},{1,5},{5... | collective-permute-start | bytes 6291464 | tf_op jit(solution)/shard_map/ppermute | solution.py:89
  178.4 26.7 %collective-permute-start.4 = (bf16[256,4096]{1,0:T(8,128)(2,1)}, bf16[256,4096]{1,0:T(8,128)(2,1)}, u32[]{:S(2)}, u32[]{:S(2)}) collective-permute-start(bf16[256,4096]{1,0:T(8,128)(2,1)} %collective-permute-done.3), channel_id=1, source_target_pairs={{0,4},{4,8},{8,12},{12,16},{16,20},{20,24},{24,28},{28,0},{1,5},{5... | collective-permute-start | bytes 6291464 | tf_op jit(solution)/shard_map/ppermute | solution.py:89
  205.0 37.2 %collective-permute-start.5 = (bf16[256,4096]{1,0:T(8,128)(2,1)}, bf16[256,4096]{1,0:T(8,128)(2,1)}, u32[]{:S(2)}, u32[]{:S(2)}) collective-permute-start(bf16[256,4096]{1,0:T(8,128)(2,1)} %collective-permute-done.4), channel_id=1, source_target_pairs={{0,4},{4,8},{8,12},{12,16},{16,20},{20,24},{24,28},{28,0},{1,5},{5... | collective-permute-start | bytes 6291464 | tf_op jit(solution)/shard_map/ppermute | solution.py:89
  239.7 1.9 copy-start
  239.7 2.2 copy-start.4
  241.6 1.7 copy-start.2
  242.2 26.6 %collective-permute-start.6 = (bf16[256,4096]{1,0:T(8,128)(2,1)}, bf16[256,4096]{1,0:T(8,128)(2,1)S(1)}, u32[]{:S(2)}, u32[]{:S(2)}) collective-permute-start(bf16[256,4096]{1,0:T(8,128)(2,1)} %collective-permute-done.5), channel_id=1, source_target_pairs={{0,4},{4,8},{8,12},{12,16},{16,20},{20,24},{24,28},{28,0},{1,5},{5... | collective-permute-start | bytes 6291464 | tf_op jit(solution)/shard_map/ppermute | solution.py:89
  245.4 23.7 %slice-start = ((s8[8388608]{0:T(1024)(128)(4,1)}), s8[4194304]{0:T(1024)(128)(4,1)S(1)}, s32[]{:S(2)}) async-start(s8[8388608]{0:T(1024)(128)(4,1)} %bitcast.26), calls=%async_computation.1 | async-start | bytes 8388608
  249.3 19.8 %slice-start.1 = ((s8[8388608]{0:T(1024)(128)(4,1)}), s8[4194304]{0:T(1024)(128)(4,1)S(1)}, s32[]{:S(2)}) async-start(s8[8388608]{0:T(1024)(128)(4,1)} %bitcast.26), calls=%async_computation.2 | async-start | bytes 8388608
Sparse Core Ops, SparseCore 0:
  22.3 48.6 all-gather.1
